TPU v7x, 32 devices: a whole 2x2x4 slice. The times are simulated.
32 devices in a mesh: groups: 2 (over y), dp: 4 (over z), pipe: 2 (over x), sub: 2 (over core).
Axes of the slice: x: 2, y: 2, z: 4, core: 2. Of those that a mesh axis runs over, the one named last changes fastest.
Arguments:
- tokens: bfloat16 [2, 2048, 8192], P('pipe', ('groups', 'dp'), 'sub'), parts along dimension 1, may hold values from -6 to 6
- cotangent: bfloat16 [2, 2048, 2, 1024], P('pipe', ('groups', 'dp')), parts along dimension 1, may hold values from -0.125 to 0.125
- frozen_weight: bfloat16 [2, 2, 1024, 8192], P('pipe', None, None, ('sub', 'dp')), may hold values from -0.0625 to 0.0625
- adapter_down: float32 [2, 64, 4, 8192], P('pipe', 'dp', 'groups', 'sub'), parts along dimension 2, may hold values from -0.0625 to 0.0625
- down_first_moment: float32 [2, 64, 4, 8192], P('pipe', 'dp', 'groups', 'sub'), parts along dimension 2, may hold values from -3 to 3
- down_second_moment: float32 [2, 64, 4, 8192], P('pipe', 'dp', 'groups', 'sub'), parts along dimension 2, may hold values from 0.05 to 2
- adapter_up: float32 [2, 1024, 4, 64], P('pipe', 'dp', 'groups'), parts along dimension 2, may hold values from -0.1875 to 0.1875
- up_first_moment: float32 [2, 1024, 4, 64], P('pipe', 'dp', 'groups'), parts along dimension 2, may hold values from -3 to 3
- up_second_moment: float32 [2, 1024, 4, 64], P('pipe', 'dp', 'groups'), parts along dimension 2, may hold values from 0.05 to 2
Outputs:
- merged_weight: bfloat16 [2, 4, 1024, 8192], P('pipe', 'groups', None, ('sub', 'dp')), parts along dimension 1
- new_down: float32 [2, 64, 4, 8192], P('pipe', 'dp', 'groups', 'sub'), parts along dimension 2
- new_down_moment: float32 [2, 64, 4, 8192], P('pipe', 'dp', 'groups', 'sub'), parts along dimension 2
- new_down_square: float32 [2, 64, 4, 8192], P('pipe', 'dp', 'groups', 'sub'), parts along dimension 2
- refreshed_up: float32 [2, 1024, 4, 64], P('pipe', 'dp', 'groups'), parts along dimension 2
- new_up_moment: float32 [2, 1024, 4, 64], P('pipe', 'dp', 'groups'), parts along dimension 2
- new_up_square: float32 [2, 1024, 4, 64], P('pipe', 'dp', 'groups'), parts along dimension 2
There are 2 independent parts, one for each index of `groups`. A program takes and returns all parts, laid end to end along the dimension named above; an argument that names none is the same for every part. Nothing has to cross between parts.
All inputs are finite; a program needn't handle non-finite values.
Results may differ from a plain program's by a relative error of at most 0.0044.
Values may be sent and summed in bfloat16 or wider, within the bound.
A program may use at most 64 MiB of HBM per device.

v0:
```python
import jax
import jax.numpy as jnp
from jax import lax
from jax.sharding import PartitionSpec as P

ADAM_STEP = 100


adapter_scale = 2.0
beta_one = 0.9
beta_two = 0.999
learn_rate = 0.005
adam_eps = 1e-08


def apply_adam_rule(current, moment, square, gradient):
    moment_new = beta_one * moment + (1.0 - beta_one) * gradient
    square_new = beta_two * square + (1.0 - beta_two) * gradient * gradient
    fix_first = 1.0 - beta_one**ADAM_STEP
    fix_second = 1.0 - beta_two**ADAM_STEP
    updated = current - learn_rate * (moment_new / fix_first) / (
        jnp.sqrt(square_new / fix_second) + adam_eps
    )
    return (updated, moment_new, square_new)


def local(
    tokens,
    cotangent,
    frozen_weight,
    adapter_down,
    down_first_moment,
    down_second_moment,
    adapter_up,
    up_first_moment,
    up_second_moment,
):
    inputs = tokens[0]
    upstream = cotangent[0]
    down_local_part = adapter_down[0].astype(jnp.bfloat16)
    up_local_part = adapter_up[0].astype(jnp.bfloat16)
    local_rows = down_local_part.shape[0]
    kv_rows = up_local_part.shape[0]
    partial_low = jnp.einsum(
        "td,rmd->tmr",
        inputs,
        lax.all_gather(down_local_part, "dp", axis=0, tiled=True),
        preferred_element_type=jnp.float32,
    )
    rank_product = lax.psum(partial_low.astype(jnp.bfloat16), "sub")
    block = upstream
    reverse_pass = jnp.einsum(
        "tmo,omr->tmr",
        block,
        lax.all_gather(up_local_part, "dp", axis=0, tiled=True),
        preferred_element_type=jnp.float32,
    ).astype(jnp.bfloat16)
    block = reverse_pass
    sum_down = lax.psum(
        (
            adapter_scale
            * jnp.einsum("qpj,qg->jpg", block, inputs, preferred_element_type=jnp.float32)
        ).astype(jnp.bfloat16),
        "dp",
    ).astype(jnp.float32)
    block = upstream
    sum_up = lax.psum(
        (
            adapter_scale
            * jnp.einsum("iyq,iyv->qyv", block, rank_product, preferred_element_type=jnp.float32)
        ).astype(jnp.bfloat16),
        "dp",
    ).astype(jnp.float32)
    position = lax.axis_index("dp")
    down_gradient = lax.dynamic_slice_in_dim(sum_down, position * local_rows, local_rows, 0)
    up_gradient = lax.dynamic_slice_in_dim(sum_up, position * kv_rows, kv_rows, 0)
    new_down, down_first, down_second = apply_adam_rule(
        adapter_down[0], down_first_moment[0], down_second_moment[0], down_gradient
    )
    refreshed_up, up_first_estimate, up_second_estimate = apply_adam_rule(
        adapter_up[0], up_first_moment[0], up_second_moment[0], up_gradient
    )
    down_cast = new_down.astype(jnp.bfloat16)
    up_cast = refreshed_up.astype(jnp.bfloat16)
    columns = lax.all_to_all(down_cast, "dp", split_axis=2, concat_axis=0, tiled=True)
    weight_change = jnp.einsum(
        "omr,rmd->mod",
        lax.all_gather(up_cast, "dp", axis=0, tiled=True),
        columns,
        preferred_element_type=jnp.float32,
    )
    combined_weight = (frozen_weight[0].astype(jnp.float32) + adapter_scale * weight_change).astype(
        jnp.bfloat16
    )
    return (
        combined_weight[None],
        new_down[None],
        down_first[None],
        down_second[None],
        refreshed_up[None],
        up_first_estimate[None],
        up_second_estimate[None],
    )


def solution(mesh):
    return jax.shard_map(
        local,
        mesh=mesh,
        in_specs=(
            P("pipe", ("groups", "dp"), "sub"),
            P("pipe", ("groups", "dp"), None, None),
            P("pipe", None, None, ("sub", "dp")),
            P("pipe", "dp", "groups", "sub"),
            P("pipe", "dp", "groups", "sub"),
            P("pipe", "dp", "groups", "sub"),
            P("pipe", "dp", "groups", None),
            P("pipe", "dp", "groups", None),
            P("pipe", "dp", "groups", None),
        ),
        out_specs=(
            P("pipe", "groups", None, ("sub", "dp")),
            P("pipe", "dp", "groups", "sub"),
            P("pipe", "dp", "groups", "sub"),
            P("pipe", "dp", "groups", "sub"),
            P("pipe", "dp", "groups", None),
            P("pipe", "dp", "groups", None),
            P("pipe", "dp", "groups", None),
        ),
        check_vma=False,
    )
```

profile of v0, /device:TPU:0, one launch (start us, length us, event | category | flops | bytes accessed | tf_op | source)
XLA Modules:
  0.0 181.5 jit_solution(4799400331475183016)
XLA Ops:
  7.2 0.0 copy-start
  7.2 0.0 copy-start.1
  7.2 0.0 all-gather.2.cloned.1.call-start
  7.2 2.2 %copy.53 = bf16[1,16,2,4096]{3,1,2,0:T(8,128)(2,1)} copy(f32[1,16,2,4096]{3,2,1,0:T(2,128)} %param.12) | data formatting | bytes 786432 | tf_op args[3]
  9.4 0.0 all-gather.2.cloned.1.call-update
  9.5 0.0 all-reduce.4.cloned.1.call-start
  9.5 2.4 %copy.33 = bf16[256,2,1024]{0,2,1:T(8,128)(2,1)S(1)} copy(bf16[256,2,1024]{2,1,0:T(2,128)(2,1)} %bitcast.91) | data formatting | bytes 2097152 | tf_op jit(solution)/shard_map/squeeze | solution.py:39
  11.9 0.0 copy-done.1
  12.0 17.2 %all_gather.11 = bf16[1024,2,64]{0,2,1:T(8,128)(2,1)S(1)} all-gather(bf16[256,2,64]{0,2,1:T(8,128)(2,1)S(1)} %bitcast_convert_fusion.1), channel_id=1, replica_groups=mesh['groups'=2,'dp'=4,'pipe'=2,'sub'=2] {'dp'}, dimensions={0}, use_global_device_ids=true | all-gather | bytes 327680 | tf_op jit(solution)/shard_map/all_gather | solution.py:55
  29.2 13.3 %all-gather.2.cloned.1.call-done = bf16[64,2,4096]{2,0,1:T(8,128)(2,1)} async-done(((bf16[16,2,4096]{2,0,1:T(8,128)(2,1)}), bf16[64,2,4096]{2,0,1:T(8,128)(2,1)}) %all-gather.2.cloned.1.call-update) | async-done | bytes 1048592 | tf_op jit(solution)/shard_map/all_gather | solution.py:47
  42.4 0.0 copy-done
  42.4 2.7 %fusion.13 = bf16[256,2,64]{0,2,1:T(8,128)(2,1)} fusion(bf16[64,2,4096]{2,0,1:T(8,128)(2,1)} %all-gather.2.cloned.1.call-done, bf16[1,256,4096]{2,1,0:T(8,128)(2,1)S(1)} %copy-done), kind=kOutput, calls=%fused_computation.15 | convolution fusion | flops 268468224 | bytes 3211264 | tf_op jit(solution)/shard_map/td,rmd->tmr/dot_general | solution.py:44
  45.1 0.0 all-reduce.4.cloned.1.call-update
  45.1 0.0 all-reduce.6.cloned.1.call-start
  45.2 1.7 fusion.2
  46.9 15.9 %all-reduce.4.cloned.1.call-done = bf16[256,2,64]{0,2,1:T(8,128)(2,1)} async-done(((bf16[256,2,64]{0,2,1:T(8,128)(2,1)}), bf16[256,2,64]{0,2,1:T(8,128)(2,1)}) %all-reduce.4.cloned.1.call-update) | async-done | bytes 65552 | tf_op jit(solution)/shard_map/psum | solution.py:50
  62.7 2.0 %fusion.8 = bf16[1024,2,64]{0,2,1:T(8,128)(2,1)} fusion(bf16[256,2,64]{0,2,1:T(8,128)(2,1)} %all-reduce.4.cloned.1.call-done, bf16[256,2,1024]{0,2,1:T(8,128)(2,1)S(1)} %copy.33), kind=kOutput, calls=%fused_computation.11 | convolution fusion | flops 67371008 | bytes 1376256 | tf_op jit(solution)/shard_map/iyq,iyv->qyv/dot_general | solution.py:70
  64.7 0.0 all-reduce.6.cloned.1.call-update
  64.8 62.5 %all-reduce.6.cloned.1.call-done = (bf16[1024,2,64]{0,2,1:T(8,128)(2,1)}, bf16[64,2,4096]{2,0,1:T(8,128)(2,1)}) async-done(((bf16[1024,2,64]{0,2,1:T(8,128)(2,1)}, bf16[64,2,4096]{2,0,1:T(8,128)(2,1)}), (bf16[1024,2,64]{0,2,1:T(8,128)(2,1)}, bf16[64,2,4096]{2,0,1:T(8,128)(2,1)})) %all-reduce.6.cloned.1.call-update) | async-done | bytes 1310736 | tf_op jit(solution)/shard_map/psum | solution.py:67
  127.3 3.3 %fusion.24 = (bf16[16,2,4096]{2,0,1:T(8,128)(2,1)S(1)}, f32[16,2,4096]{2,0,1:T(8,128)}, f32[1,16,2,4096]{3,1,2,0:T(8,128)S(1)}, f32[1,16,2,4096]{3,1,2,0:T(8,128)S(1)}) fusion(f32[1,16,2,4096]{3,2,1,0:T(2,128)} %param.14, bf16[64,2,4096]{2,0,1:T(8,128)(2,1)} %get-tuple-element.22, s32[]{:T(128)S(6)} %select_n.7, f32[1,16,2,4096]{3,2,1,0:T(2,128)} %param.13, ...), kind=kLoop, calls=%fused_computation.34 | loop fusion | flops 1835008 | bytes 3670020 | tf_op jit(solution)/shard_map/convert_element_type | solution.py:83
  130.6 3.8 %copy.28 = bf16[16,2,4096]{0,1,2:T(2,128)(2,1)} copy(bf16[16,2,4096]{2,0,1:T(8,128)(2,1)S(1)} %get-tuple-element.23) | data formatting | bytes 524288 | tf_op jit(solution)/shard_map/convert_element_type | solution.py:83
  134.4 4.0 %reshape.26 = bf16[4,2,16384]{2,1,0:T(2,128)(2,1)} reshape(bf16[4096,2,16]{2,1,0:T(2,128)(2,1)} %bitcast.86) | data formatting | bytes 524288
  138.4 3.4 %all-to-all-start = ((bf16[4,2,16384]{2,1,0:T(2,128)(2,1)}), bf16[4,2,16384]{2,1,0:T(2,128)(2,1)S(1)}, u32[]{:S(2)}, u32[]{:S(2)}) async-start(bf16[4,2,16384]{2,1,0:T(2,128)(2,1)} %reshape.26), calls=%async_computation | async-start | bytes 524288 | tf_op jit(solution)/shard_map/all_to_all | solution.py:85
  141.9 0.0 copy-start.2
  141.9 0.0 copy-start.3
  141.9 2.3 %copy.30 = f32[1,16,2,4096]{3,2,1,0:T(2,128)} copy(f32[1,16,2,4096]{3,1,2,0:T(8,128)} %bitcast.88) | data formatting | bytes 1048576
  144.2 1.2 copy.32
  145.4 1.2 copy.31
  146.6 0.0 copy-done.2
  146.6 0.0 copy-done.3
  146.6 1.6 fusion.25
  148.2 14.4 %all_gather.10 = bf16[1024,2,64]{0,2,1:T(8,128)(2,1)S(1)} all-gather(bf16[256,2,64]{0,2,1:T(8,128)(2,1)S(1)} %get-tuple-element.25), channel_id=1, replica_groups=mesh['groups'=2,'dp'=4,'pipe'=2,'sub'=2] {'dp'}, dimensions={0}, use_global_device_ids=true | all-gather | bytes 327680 | tf_op jit(solution)/shard_map/all_gather | solution.py:88
  162.6 0.0 all-to-all-done
  162.6 2.4 %reshape.27 = bf16[4096,2,16]{2,1,0:T(2,128)(2,1)} reshape(bf16[4,2,16384]{2,1,0:T(2,128)(2,1)S(1)} %all-to-all-done) | data formatting | bytes 524288
  165.0 4.5 %copy.29 = bf16[16,2,4,1024]{3,0,2,1:T(8,128)(2,1)S(1)} copy(bf16[16,2,4,1024]{0,1,3,2:T(2,128)(2,1)} %bitcast.87) | data formatting | bytes 524288 | tf_op jit(solution)/shard_map/all_to_all | solution.py:85
  169.5 5.5 %fusion.3 = bf16[1,2,1024,1024]{3,2,1,0:T(8,128)(2,1)} fusion(bf16[1,2,1024,1024]{3,2,1,0:T(8,128)(2,1)} %param.11, bf16[1024,2,64]{0,2,1:T(8,128)(2,1)S(1)} %all_gather.10, bf16[64,2,1024]{2,0,1:T(8,128)(2,1)S(1)} %bitcast.89), kind=kOutput, calls=%fused_computation.5 | convolution fusion | flops 276824064 | bytes 8912896 | tf_op jit(solution)/shard_map/omr,rmd->mod/dot_general | solution.py:86
  (1 shorter events, 0.0 us)
Async XLA Ops:
  7.2 35.3 %copy-start = (bf16[1,256,4096]{2,1,0:T(8,128)(2,1)S(1)}, bf16[1,256,4096]{2,1,0:T(8,128)(2,1)}, u32[]{:S(2)}) copy-start(bf16[1,256,4096]{2,1,0:T(8,128)(2,1)} %param.9) | copy-start | bytes 6291460
  7.2 4.7 %copy-start.1 = (f32[1,256,2,64]{1,3,2,0:T(8,128)S(1)}, f32[1,256,2,64]{1,3,2,0:T(8,128)}, u32[]{:S(2)}) copy-start(f32[1,256,2,64]{1,3,2,0:T(8,128)} %param.15) | copy-start | bytes 393220
  7.2 35.2 %all-gather.2.cloned.1.call-start = ((), (), s32[]{:S(2)}) async-start(), calls=%async_computation.1 | async-start | bytes 1310720 | tf_op jit(solution)/shard_map/all_gather | solution.py:47
  9.5 53.3 %all-reduce.4.cloned.1.call-start = ((), (), s32[]{:S(2)}) async-start(), calls=%async_computation.2 | async-start | bytes 131072 | tf_op jit(solution)/shard_map/psum | solution.py:50
  45.1 82.1 %all-reduce.6.cloned.1.call-start = ((), (), s32[]{:S(2)}) async-start(), calls=%async_computation.3 | async-start | bytes 2621440 | tf_op jit(solution)/shard_map/psum | solution.py:67
  138.4 24.2 %all-to-all-start = ((bf16[4,2,16384]{2,1,0:T(2,128)(2,1)}), bf16[4,2,16384]{2,1,0:T(2,128)(2,1)S(1)}, u32[]{:S(2)}, u32[]{:S(2)}) async-start(bf16[4,2,16384]{2,1,0:T(2,128)(2,1)} %reshape.26), calls=%async_computation | async-start | bytes 524288 | tf_op jit(solution)/shard_map/all_to_all | solution.py:85
  141.9 4.7 %copy-start.2 = (f32[1,256,2,64]{1,3,2,0:T(8,128)S(1)}, f32[1,256,2,64]{1,3,2,0:T(8,128)}, u32[]{:S(2)}) copy-start(f32[1,256,2,64]{1,3,2,0:T(8,128)} %param.17) | copy-start | bytes 393220
  141.9 4.7 %copy-start.3 = (f32[1,256,2,64]{1,3,2,0:T(8,128)S(1)}, f32[1,256,2,64]{1,3,2,0:T(8,128)}, u32[]{:S(2)}) copy-start(f32[1,256,2,64]{1,3,2,0:T(8,128)} %param.16) | copy-start | bytes 393220
Sparse Core Ops, SparseCore 0:
  10.2 32.2 all-gather.1
  45.3 17.4 all-reduce.3
  65.8 61.4 all-reduce.5
where the time goes:
time: 182 us
  waiting for transfers between devices  91.7 us (50%)
  blocking collectives  31.6 us (17%)
  local copies, waits for them, and re-layouts  24 us (13%)
  between operations  13.8 us (8%)
  matrix products  11.9 us (7%)
  other arithmetic  4.98 us (3%)
  starting transfers between devices  3.53 us (2%)
    psum x1, waiting for transfers between devices, local(): lax.psum((adapter_scale * jnp.einsum('iyq,iyv->qyv', block, rank_product,...  62.5 us
    all_gather x1, blocking collectives, local(): lax.all_gather(up_local_part, 'dp', axis=0, tiled=True)  17.2 us
    psum x1, waiting for transfers between devices, local(): rank_product = lax.psum(partial_low.astype(jnp.bfloat16), 'sub')  15.9 us
    all_gather x1, blocking collectives, local(): lax.all_gather(up_cast, 'dp', axis=0, tiled=True)  14.4 us
    unnamed x14, local copies, waits for them, and re-layouts  13.3 us
    all_gather x1, waiting for transfers between devices, local(): lax.all_gather(down_local_part, 'dp', axis=0, tiled=True)  13.3 us
    dot_general x1, matrix products, local(): jnp.einsum('omr,rmd->mod', lax.all_gather(up_cast, 'dp', axis=0, tiled=Tr...  5.5 us
    all_to_all x1, local copies, waits for them, and re-layouts, local(): lax.all_to_all(down_cast, 'dp', split_axis=2, concat_axis=0, tiled=True)  4.5 us
  transfers between devices with their start and end apart: 4, of which 3 were waited for; matrix products, arithmetic and copies ran while one was open for 6% of the time, Pallas kernels for 0%

commit v1 on v0

v1 whole, which is shorter than its diff:
```python
import functools

import jax
import jax.numpy as jnp
from jax import lax
from jax.experimental import pallas as pl
from jax.experimental.pallas import tpu as pltpu
from jax.sharding import PartitionSpec as P

ADAM_STEP = 100

adapter_scale = 2.0
beta_one = 0.9
beta_two = 0.999
learn_rate = 0.005
adam_eps = 1e-08

MESH = pl.DeviceIdType.MESH
UP, UP_CROSS, DOWN, GRAD_DOWN, LOW, GRAD_UP, NEW_UP, NEW_UP_CROSS, STATE, COLUMNS = range(10)
KINDS = 10


def apply_adam_rule(current, moment, square, gradient):
    moment_new = beta_one * moment + (1.0 - beta_one) * gradient
    square_new = beta_two * square + (1.0 - beta_two) * gradient * gradient
    fix_first = 1.0 - beta_one**ADAM_STEP
    fix_second = 1.0 - beta_two**ADAM_STEP
    updated = current - learn_rate * (moment_new / fix_first) / (
        jnp.sqrt(square_new / fix_second) + adam_eps
    )
    return (updated, moment_new, square_new)


def exchange_kernel(
    n,
    tok_hbm, cot_hbm, down, first_hbm, second_hbm, up, up_first, up_second,
    new_down, new_first, new_second, new_up, new_up_first, new_up_second, columns_out, up_out,
    tok, cot_raw, cot, first, second,
    up_all, down_all, back, grad_send, grad_recv, grad_own,
    low_own, low_send, low_recv, gu_send, gu_recv, gu_own, up_new_all, state, col_send, col_all,
    sems, local_sems,
):
    bf16, f32 = jnp.bfloat16, jnp.float32
    me = lax.axis_index("dp")
    core = lax.axis_index("sub")
    other = 1 - core
    rows = down.shape[0]
    rank = up.shape[1]
    kv_rows = up.shape[2]
    width = down.shape[2] // n

    def ahead(k):
        return lax.rem(me + k, n)

    def behind(k):
        return lax.rem(me + n - k, n)

    def to_learner(kind, k, src, dst):
        return pltpu.make_async_remote_copy(
            src_ref=src, dst_ref=dst,
            send_sem=sems.at[kind, 0, k], recv_sem=sems.at[kind, 1, k],
            device_id={"dp": ahead(k)}, device_id_type=MESH,
        )

    def to_core(kind, k, src, dst):
        return pltpu.make_async_remote_copy(
            src_ref=src, dst_ref=dst,
            send_sem=sems.at[kind, 0, k], recv_sem=sems.at[kind, 1, k],
            device_id={"sub": other}, device_id_type=MESH,
        )

    def loop(lo, hi, body):
        if n <= 4:
            for k in range(lo, hi):
                body(k)
        else:
            lax.fori_loop(lo, hi, lambda k, c: (body(k), c)[1], 0)

    locals_ = [
        pltpu.make_async_copy(src, dst, local_sems.at[i])
        for i, (src, dst) in enumerate(
            ((cot_hbm, cot_raw), (tok_hbm, tok), (first_hbm, first), (second_hbm, second))
        )
    ]
    for c in locals_:
        c.start()

    barrier = pltpu.get_barrier_semaphore()
    loop(1, n, lambda k: pl.semaphore_signal(
        barrier, inc=1, device_id={"dp": ahead(k)}, device_id_type=MESH))
    pl.semaphore_signal(barrier, inc=1, device_id={"sub": other}, device_id_type=MESH)

    up_all[me] = up[...].astype(bf16)
    for m in range(2):
        down_all[me, m] = down[:, m, :].astype(bf16)

    pl.semaphore_wait(barrier, n)

    def send_up(k):
        block = up_all.at[me, core]
        to_learner(UP, k, block, block).start()

    def send_down(k):
        block = down_all.at[me]
        to_learner(DOWN, k, block, block).start()

    loop(1, n, send_up)
    loop(1, n, send_down)

    locals_[0].wait()
    for m in range(2):
        cot[m] = cot_raw[:, m, :]

    def pass_up(k):
        block = up_all.at[behind(k), core]
        to_learner(UP, k, block, block).wait_recv()
        to_core(UP_CROSS, k, block, block).start()

    loop(1, n, pass_up)

    def got_up(k):
        block = up_all.at[behind(k), other]
        to_core(UP_CROSS, k, block, block).wait_recv()

    loop(1, n, got_up)

    for m in range(2):
        total = jnp.zeros((rank, tok.shape[0]), f32)
        for q in range(n):
            total = total + lax.dot_general(
                up_all[q, m], cot[m, :, q * kv_rows:(q + 1) * kv_rows],
                (((1,), (1,)), ((), ())), preferred_element_type=f32)
        total = total.astype(bf16)
        for q in range(n):
            back[q, m] = total[q * rows:(q + 1) * rows]

    locals_[1].wait()

    def grad_for(q):
        lhs = back[q].reshape(2 * rows, tok.shape[0])
        return adapter_scale * jnp.dot(lhs, tok[...], preferred_element_type=f32)

    def send_grad(k):
        q = ahead(k)
        g = grad_for(q).astype(bf16)
        grad_send[k, 0] = g[:rows]
        grad_send[k, 1] = g[rows:]
        to_learner(GRAD_DOWN, k, grad_send.at[k], grad_recv.at[k]).start()

    loop(1, n, send_grad)
    g = grad_for(me)
    grad_own[0] = g[:rows]
    grad_own[1] = g[rows:]

    def low_for(q):
        part = lax.dot_general(
            down_all[q].reshape(2 * rows, tok.shape[1]), tok[...],
            (((1,), (1,)), ((), ())), preferred_element_type=f32)
        for m in range(2):
            low_own[m, q] = part[m * rows:(m + 1) * rows]
            low_send[m, q] = part[m * rows:(m + 1) * rows].astype(bf16)

    low_for(me)

    def take_down(k):
        q = behind(k)
        block = down_all.at[q]
        to_learner(DOWN, k, block, block).wait_recv()
        low_for(q)

    loop(1, n, take_down)
    half = to_core(LOW, 0, low_send.at[other], low_recv)
    half.start()
    half.wait()
    lowrank = (low_own[core] + low_recv[...].astype(f32)).astype(bf16).reshape(rank, tok.shape[0])

    gu = adapter_scale * jnp.dot(lowrank, cot[core], preferred_element_type=f32)
    for q in range(n):
        gu_own[q] = gu[:, q * kv_rows:(q + 1) * kv_rows]
        gu_send[q] = gu[:, q * kv_rows:(q + 1) * kv_rows].astype(bf16)

    loop(1, n, lambda k: to_learner(GRAD_UP, k, gu_send.at[ahead(k)], gu_recv.at[k]).start())
    gu_own[n] = gu_own[me]

    def add_up(k):
        to_learner(GRAD_UP, k, gu_send.at[ahead(k)], gu_recv.at[k]).wait_recv()
        gu_own[n] = gu_own[n] + gu_recv[k].astype(f32)

    loop(1, n, add_up)
    p, f, s = apply_adam_rule(up[core], up_first[core], up_second[core], gu_own[n])
    up_new_all[me, core] = p.astype(bf16)

    def send_new_up(k):
        block = up_new_all.at[me, core]
        to_learner(NEW_UP, k, block, block).start()

    loop(1, n, send_new_up)
    state[core, 0] = p
    state[core, 1] = f
    state[core, 2] = s
    mine = to_core(STATE, 0, state.at[core], state.at[core])
    mine.start()

    locals_[2].wait()
    locals_[3].wait()
    loop(1, n, lambda k: to_learner(
        GRAD_DOWN, k, grad_send.at[k], grad_recv.at[k]).wait_recv())

    def adam_down(k):
        q = ahead(k)
        cols = pl.ds(pl.multiple_of(q * width, 128), width)
        for m in range(2):
            g = grad_own[m, :, cols]
            for j in range(1, n):
                g = g + grad_recv[j, m, :, cols].astype(f32)
            p, f, s = apply_adam_rule(down[:, m, cols], first[:, m, cols], second[:, m, cols], g)
            new_down[:, m, cols] = p
            new_first[:, m, cols] = f
            new_second[:, m, cols] = s
            if isinstance(k, int) and k == 0:
                col_all[me, m] = p.astype(bf16)
            else:
                col_send[k, m] = p.astype(bf16)

    def send_columns(k):
        adam_down(k)
        to_learner(COLUMNS, k, col_send.at[k], col_all.at[me]).start()

    loop(1, n, send_columns)
    adam_down(0)

    def pass_new_up(k):
        block = up_new_all.at[behind(k), core]
        to_learner(NEW_UP, k, block, block).wait_recv()
        to_core(NEW_UP_CROSS, k, block, block).start()

    loop(1, n, pass_new_up)
    to_core(STATE, 0, state.at[other], state.at[other]).wait_recv()
    for m in range(2):
        new_up[m] = state[m, 0]
        new_up_first[m] = state[m, 1]
        new_up_second[m] = state[m, 2]
    up_new_all[me, other] = state[other, 0].astype(bf16)

    def got_new_up(k):
        block = up_new_all.at[behind(k), other]
        to_core(NEW_UP_CROSS, k, block, block).wait_recv()

    loop(1, n, got_new_up)
    for m in range(2):
        for q in range(n):
            up_out[m, :, q * kv_rows:(q + 1) * kv_rows] = up_new_all[q, m]

    def got_columns(k):
        to_learner(COLUMNS, k, col_send.at[k], col_all.at[behind(k)]).wait_recv()

    loop(1, n, got_columns)
    for m in range(2):
        for q in range(n):
            columns_out[m, q * rows:(q + 1) * rows, :] = col_all[q, m]

    def sent(k):
        block = up_all.at[me, core]
        to_learner(UP, k, block, block).wait_send()
        block = up_all.at[behind(k), core]
        to_core(UP_CROSS, k, block, block).wait_send()
        block = down_all.at[me]
        to_learner(DOWN, k, block, block).wait_send()
        to_learner(GRAD_DOWN, k, grad_send.at[k], grad_recv.at[k]).wait_send()
        to_learner(GRAD_UP, k, gu_send.at[ahead(k)], gu_recv.at[k]).wait_send()
        block = up_new_all.at[me, core]
        to_learner(NEW_UP, k, block, block).wait_send()
        block = up_new_all.at[behind(k), core]
        to_core(NEW_UP_CROSS, k, block, block).wait_send()
        to_learner(COLUMNS, k, col_send.at[k], col_all.at[me]).wait_send()

    loop(1, n, sent)
    mine.wait_send()


def merge_kernel(
    frozen, up, columns, d0, d1, d2, u0, u1, u2,
    merged, e0, e1, e2, v0, v1, v2, sems,
):
    step = pl.program_id(0) * pl.num_programs(1) + pl.program_id(1)
    last = pl.num_programs(0) * pl.num_programs(1) - 1
    pairs = ((d0, e0), (d1, e1), (d2, e2), (u0, v0), (u1, v1), (u2, v2))
    copies = [pltpu.make_async_copy(a, b, sems.at[i]) for i, (a, b) in enumerate(pairs)]

    @pl.when(step == 0)
    def _():
        for c in copies:
            c.start()

    change = lax.dot_general(
        up[0], columns[0], (((0,), (0,)), ((), ())), preferred_element_type=jnp.float32)
    merged[0] = (frozen[0].astype(jnp.float32) + adapter_scale * change).astype(merged.dtype)

    @pl.when(step == last)
    def _():
        for c in copies:
            c.wait()


def local(
    n,
    tokens,
    cotangent,
    frozen_weight,
    adapter_down,
    down_first_moment,
    down_second_moment,
    adapter_up,
    up_first_moment,
    up_second_moment,
):
    bf16, f32 = jnp.bfloat16, jnp.float32
    tok, cot, frozen = tokens[0], cotangent[0], frozen_weight[0]
    down, first, second = adapter_down[0], down_first_moment[0], down_second_moment[0]
    up, up_first, up_second = [
        jnp.transpose(a[0], (1, 2, 0)) for a in (adapter_up, up_first_moment, up_second_moment)
    ]
    t, d = tok.shape
    _, kinds, o = cot.shape
    r = down.shape[0]
    rank, c = up.shape[1:]
    w = d // n
    vmem = pl.BlockSpec(memory_space=pltpu.VMEM)
    anywhere = pl.BlockSpec(memory_space=pl.ANY)
    down_like = jax.ShapeDtypeStruct(down.shape, f32)
    up_like = jax.ShapeDtypeStruct(up.shape, f32)
    outs = pl.pallas_call(
        functools.partial(exchange_kernel, n),
        out_shape=(
            down_like, down_like, down_like, up_like, up_like, up_like,
            jax.ShapeDtypeStruct((2, rank, w), bf16),
            jax.ShapeDtypeStruct((2, rank, o), bf16),
        ),
        in_specs=[anywhere, anywhere, vmem, anywhere, anywhere, vmem, vmem, vmem],
        out_specs=(vmem,) * 8,
        scratch_shapes=[
            pltpu.VMEM((t, d), bf16),
            pltpu.VMEM((t, 2, o), bf16),
            pltpu.VMEM((2, t, o), bf16),
            pltpu.VMEM((r, 2, d), f32),
            pltpu.VMEM((r, 2, d), f32),
            pltpu.VMEM((n, 2, rank, c), bf16),
            pltpu.VMEM((n, 2, r, d), bf16),
            pltpu.VMEM((n, 2, r, t), bf16),
            pltpu.VMEM((n, 2, r, d), bf16),
            pltpu.VMEM((n, 2, r, d), bf16),
            pltpu.VMEM((2, r, d), f32),
            pltpu.VMEM((2, n, r, t), f32),
            pltpu.VMEM((2, n, r, t), bf16),
            pltpu.VMEM((n, r, t), bf16),
            pltpu.VMEM((n, rank, c), bf16),
            pltpu.VMEM((n, rank, c), bf16),
            pltpu.VMEM((n + 1, rank, c), f32),
            pltpu.VMEM((n, 2, rank, c), bf16),
            pltpu.VMEM((2, 3, rank, c), f32),
            pltpu.VMEM((n, 2, r, w), bf16),
            pltpu.VMEM((n, 2, r, w), bf16),
            pltpu.SemaphoreType.DMA((KINDS, 2, n)),
            pltpu.SemaphoreType.DMA((4,)),
        ],
        compiler_params=pltpu.CompilerParams(
            collective_id=0, has_side_effects=True, vmem_limit_bytes=48 * 1024 * 1024
        ),
        cost_estimate=pl.CostEstimate(flops=10**9, bytes_accessed=10**7, transcendentals=0),
    )(tok, cot, down, first, second, up, up_first, up_second)
    columns, up_cast = outs[6], outs[7]
    block = min(256, o)
    merged, *rest = pl.pallas_call(
        merge_kernel,
        grid=(2, o // block),
        out_shape=(
            jax.ShapeDtypeStruct((2, o, w), bf16),
            down_like, down_like, down_like, up_like, up_like, up_like,
        ),
        in_specs=[
            pl.BlockSpec((1, block, w), lambda m, i: (m, i, 0)),
            pl.BlockSpec((1, rank, block), lambda m, i: (m, 0, i)),
            pl.BlockSpec((1, rank, w), lambda m, i: (m, 0, 0)),
        ] + [anywhere] * 6,
        out_specs=(pl.BlockSpec((1, block, w), lambda m, i: (m, i, 0)),) + (anywhere,) * 6,
        scratch_shapes=[pltpu.SemaphoreType.DMA((6,))],
        compiler_params=pltpu.CompilerParams(vmem_limit_bytes=32 * 1024 * 1024),
    )(frozen, up_cast, columns, *outs[:6])
    return (
        merged[None],
        rest[0][None],
        rest[1][None],
        rest[2][None],
        jnp.transpose(rest[3], (2, 0, 1))[None],
        jnp.transpose(rest[4], (2, 0, 1))[None],
        jnp.transpose(rest[5], (2, 0, 1))[None],
    )


def solution(mesh):
    return jax.shard_map(
        functools.partial(local, mesh.shape["dp"]),
        mesh=mesh,
        in_specs=(
            P("pipe", ("groups", "dp"), "sub"),
            P("pipe", ("groups", "dp"), None, None),
            P("pipe", None, None, ("sub", "dp")),
            P("pipe", "dp", "groups", "sub"),
            P("pipe", "dp", "groups", "sub"),
            P("pipe", "dp", "groups", "sub"),
            P("pipe", "dp", "groups", None),
            P("pipe", "dp", "groups", None),
            P("pipe", "dp", "groups", None),
        ),
        out_specs=(
            P("pipe", "groups", None, ("sub", "dp")),
            P("pipe", "dp", "groups", "sub"),
            P("pipe", "dp", "groups", "sub"),
            P("pipe", "dp", "groups", "sub"),
            P("pipe", "dp", "groups", None),
            P("pipe", "dp", "groups", None),
            P("pipe", "dp", "groups", None),
        ),
        check_vma=False,
    )
```

time: 182 us -> 79.3 us (0.44)
  waiting for transfers between devices: 91.7 us -> 0 us
  Pallas kernels: 0 us -> 70.9 us
  blocking collectives: 31.6 us -> 0 us
  local copies, waits for them, and re-layouts: 24 us -> 7.4 us
  between operations: 13.8 us -> 0.67 us
  matrix products: 11.9 us -> 0 us
  other arithmetic: 4.98 us -> 0 us
  starting transfers between devices: 3.53 us -> 0 us
    psum x2 -> x0, waiting for transfers between devices: 78.4 us -> none  [the longest x1 62.5 us: local(): lax.psum((adapter_scale * jnp.einsum('iyq,iyv->qyv', block, rank_product,...]
    pallas_call x0 -> x2, Pallas kernels: none -> 70.9 us  [the longest x1 65.6 us: local(): pl.pallas_call(functools.partial(exchange_kernel, n), out_shape=(down_lik...]
    all_gather x2 -> x0, blocking collectives: 31.6 us -> none  [the longest x1 17.2 us: local(): lax.all_gather(up_local_part, 'dp', axis=0, tiled=True)]
    all_gather x1 -> x0, waiting for transfers between devices: 13.3 us -> none  [local(): lax.all_gather(down_local_part, 'dp', axis=0, tiled=True)]
    dot_general x4 -> x0, matrix products: 11.9 us -> none  [the longest x1 5.5 us: local(): jnp.einsum('omr,rmd->mod', lax.all_gather(up_cast, 'dp', axis=0, tiled=Tr...]
    unnamed x14 -> x16, local copies, waits for them, and re-layouts: 13.3 us -> 7.4 us
    convert_element_type x3 -> x0, other arithmetic: 4.98 us -> none  [the longest x1 3.34 us: local(): down_cast = new_down.astype(jnp.bfloat16)]
    all_to_all x1 -> x0, local copies, waits for them, and re-layouts: 4.5 us -> none  [local(): lax.all_to_all(down_cast, 'dp', split_axis=2, concat_axis=0, tiled=True)]
  transfers between devices with their start and end apart: 4 -> 0, of which waited for: 3 -> 0; matrix products, arithmetic and copies ran while one was open for 6% -> 0% of each run, Pallas kernels for 0% -> 0%
where the time goes in v1:
time: 79.3 us; the launch traced here: 79 us
  Pallas kernels  70.9 us (89%)
  local copies, waits for them, and re-layouts  7.4 us (9%)
    pallas_call x1, Pallas kernels, local(): pl.pallas_call(functools.partial(exchange_kernel, n), out_shape=(down_lik...  65.6 us
    unnamed x16, local copies, waits for them, and re-layouts  7.4 us
    pallas_call x1, Pallas kernels, local(): pl.pallas_call(merge_kernel, grid=(2, o // block), out_shape=(jax.ShapeDt...  5.3 us

profile of v1, /device:TPU:0, one launch (start us, length us, event | category | flops | bytes accessed | tf_op | source)
XLA Modules:
  0.0 79.0 jit_solution(5894711354152096610)
XLA Ops:
  0.6 0.0 copy-start
  0.6 0.0 copy-start.1
  0.7 1.4 %copy-done.1 = bf16[1,256,2,1024]{3,2,1,0:T(2,128)(2,1)S(1)} copy-done((bf16[1,256,2,1024]{3,2,1,0:T(2,128)(2,1)S(1)}, bf16[1,256,2,1024]{3,2,1,0:T(2,128)(2,1)}, u32[]{:S(2)}) %copy-start.1) | copy-done | bytes 1048600
  2.0 0.0 copy-start.2
  2.0 1.2 %copy-done.2 = f32[1,16,2,4096]{3,2,1,0:T(2,128)S(1)} copy-done((f32[1,16,2,4096]{3,2,1,0:T(2,128)S(1)}, f32[1,16,2,4096]{3,2,1,0:T(2,128)}, u32[]{:S(2)}) %copy-start.2) | copy-done | bytes 524312
  3.3 0.0 copy-start.3
  3.3 1.0 %copy-done.3 = f32[1,16,2,4096]{3,2,1,0:T(2,128)S(1)} copy-done((f32[1,16,2,4096]{3,2,1,0:T(2,128)S(1)}, f32[1,16,2,4096]{3,2,1,0:T(2,128)}, u32[]{:S(2)}) %copy-start.3) | copy-done | bytes 524312
  4.3 0.0 copy-start.4
  4.3 1.0 %copy-done.4 = f32[1,16,2,4096]{3,2,1,0:T(2,128)S(1)} copy-done((f32[1,16,2,4096]{3,2,1,0:T(2,128)S(1)}, f32[1,16,2,4096]{3,2,1,0:T(2,128)}, u32[]{:S(2)}) %copy-start.4) | copy-done | bytes 524312
  5.3 0.0 copy-start.5
  5.3 0.9 %copy-done.5 = f32[1,256,2,64]{1,3,2,0:T(8,128)S(1)} copy-done((f32[1,256,2,64]{1,3,2,0:T(8,128)S(1)}, f32[1,256,2,64]{1,3,2,0:T(8,128)}, u32[]{:S(2)}) %copy-start.5) | copy-done | bytes 131096
  6.2 0.0 copy-start.6
  6.2 0.9 %copy-done.6 = f32[1,256,2,64]{1,3,2,0:T(8,128)S(1)} copy-done((f32[1,256,2,64]{1,3,2,0:T(8,128)S(1)}, f32[1,256,2,64]{1,3,2,0:T(8,128)}, u32[]{:S(2)}) %copy-start.6) | copy-done | bytes 131096
  7.1 0.0 copy-start.7
  7.2 0.9 %copy-done.7 = f32[1,256,2,64]{1,3,2,0:T(8,128)S(1)} copy-done((f32[1,256,2,64]{1,3,2,0:T(8,128)S(1)}, f32[1,256,2,64]{1,3,2,0:T(8,128)}, u32[]{:S(2)}) %copy-start.7) | copy-done | bytes 131096
  8.1 65.6 %shard_map.144 = (f32[16,2,4096]{2,1,0:T(2,128)S(1)}, f32[16,2,4096]{2,1,0:T(2,128)S(1)}, f32[16,2,4096]{2,1,0:T(2,128)S(1)}, f32[2,64,256]{2,1,0:T(8,128)S(1)},...) custom-call(bf16[256,4096]{1,0:T(8,128)(2,1)} %bitcast.36, ...), custom_call_target="tpu_custom_call" | custom-call | flops 1000000000 | bytes 10000000 | tf_op jit(solution)/shard_map/pallas_call | solution.py:332
  73.7 0.0 copy-done
  73.7 5.3 %shard_map.145 = (bf16[2,1024,1024]{2,1,0:T(8,128)(2,1)}, f32[16,2,4096]{2,1,0:T(2,128)}, f32[16,2,4096]{2,1,0:T(2,128)}, f32[16,2,4096]{2,1,0:T(2,128)}, f32[2,...) custom-call(bf16[2,1024,1024]{2,1,0:T(8,128)(2,1)S(1)} %bitcast.28, ...), custom_call_target="tpu_custom_call" | custom-call | tf_op jit(solution)/shard_map/pallas_call | solution.py:373
Async XLA Ops:
  0.6 73.1 %copy-start = (bf16[1,2,1024,1024]{3,2,1,0:T(8,128)(2,1)S(1)}, bf16[1,2,1024,1024]{3,2,1,0:T(8,128)(2,1)}, u32[]{:S(2)}) copy-start(bf16[1,2,1024,1024]{3,2,1,0:T(8,128)(2,1)} %param.11) | copy-start | bytes 12582916
  0.6 1.4 %copy-start.1 = (bf16[1,256,2,1024]{3,2,1,0:T(2,128)(2,1)S(1)}, bf16[1,256,2,1024]{3,2,1,0:T(2,128)(2,1)}, u32[]{:S(2)}) copy-start(bf16[1,256,2,1024]{3,2,1,0:T(2,128)(2,1)} %param.10) | copy-start | bytes 3145732
  2.0 1.2 %copy-start.2 = (f32[1,16,2,4096]{3,2,1,0:T(2,128)S(1)}, f32[1,16,2,4096]{3,2,1,0:T(2,128)}, u32[]{:S(2)}) copy-start(f32[1,16,2,4096]{3,2,1,0:T(2,128)} %param.12) | copy-start | bytes 1572868
  3.3 1.0 %copy-start.3 = (f32[1,16,2,4096]{3,2,1,0:T(2,128)S(1)}, f32[1,16,2,4096]{3,2,1,0:T(2,128)}, u32[]{:S(2)}) copy-start(f32[1,16,2,4096]{3,2,1,0:T(2,128)} %param.13) | copy-start | bytes 1572868
  4.3 1.0 %copy-start.4 = (f32[1,16,2,4096]{3,2,1,0:T(2,128)S(1)}, f32[1,16,2,4096]{3,2,1,0:T(2,128)}, u32[]{:S(2)}) copy-start(f32[1,16,2,4096]{3,2,1,0:T(2,128)} %param.14) | copy-start | bytes 1572868
  5.3 0.9 %copy-start.5 = (f32[1,256,2,64]{1,3,2,0:T(8,128)S(1)}, f32[1,256,2,64]{1,3,2,0:T(8,128)}, u32[]{:S(2)}) copy-start(f32[1,256,2,64]{1,3,2,0:T(8,128)} %param.15) | copy-start | bytes 393220
  6.2 0.9 %copy-start.6 = (f32[1,256,2,64]{1,3,2,0:T(8,128)S(1)}, f32[1,256,2,64]{1,3,2,0:T(8,128)}, u32[]{:S(2)}) copy-start(f32[1,256,2,64]{1,3,2,0:T(8,128)} %param.16) | copy-start | bytes 393220
  7.1 0.9 %copy-start.7 = (f32[1,256,2,64]{1,3,2,0:T(8,128)S(1)}, f32[1,256,2,64]{1,3,2,0:T(8,128)}, u32[]{:S(2)}) copy-start(f32[1,256,2,64]{1,3,2,0:T(8,128)} %param.17) | copy-start | bytes 393220

commit v2 on v1

--- a/solution.py
+++ b/solution.py
@@ -16,8 +16,8 @@
 adam_eps = 1e-08
 
 MESH = pl.DeviceIdType.MESH
-UP, UP_CROSS, DOWN, GRAD_DOWN, LOW, GRAD_UP, NEW_UP, NEW_UP_CROSS, STATE, COLUMNS = range(10)
-KINDS = 10
+UP, UP_CROSS, DOWN, GRAD_DOWN, LOW, GRAD_UP, NEW_UP, NEW_UP_CROSS, STATE, COLUMNS, RELAY = range(11)
+KINDS = 11
 
 
 def apply_adam_rule(current, moment, square, gradient):
@@ -33,12 +33,12 @@
 
 def exchange_kernel(
     n,
-    tok_hbm, cot_hbm, down, first_hbm, second_hbm, up, up_first, up_second,
+    tok_hbm, cot_hbm, down_hbm, first_hbm, second_hbm, up_hbm, up_first_hbm, up_second_hbm,
     new_down, new_first, new_second, new_up, new_up_first, new_up_second, columns_out, up_out,
-    tok, cot_raw, cot, first, second,
+    tok, cot_raw, cot, down, first, second, up, up_first, up_second,
     up_all, down_all, back, grad_send, grad_recv, grad_own,
     low_own, low_send, low_recv, gu_send, gu_recv, gu_own, up_new_all, state, col_send, col_all,
-    sems, local_sems,
+    grad_relay, sems, local_sems,
 ):
     bf16, f32 = jnp.bfloat16, jnp.float32
     me = lax.axis_index("dp")
@@ -69,6 +69,13 @@
             device_id={"sub": other}, device_id_type=MESH,
         )
 
+    relayed = n == 4
+    if relayed:
+        middle = jnp.logical_and(me > 0, me < 3)
+        toward = jnp.where(me < 2, 3, 1)
+        near = 4 - toward
+        beside = lax.rem(3 * me + 1, 4)
+
     def loop(lo, hi, body):
         if n <= 4:
             for k in range(lo, hi):
@@ -79,7 +86,11 @@
     locals_ = [
         pltpu.make_async_copy(src, dst, local_sems.at[i])
         for i, (src, dst) in enumerate(
-            ((cot_hbm, cot_raw), (tok_hbm, tok), (first_hbm, first), (second_hbm, second))
+            (
+                (up_hbm, up), (down_hbm, down), (cot_hbm, cot_raw), (tok_hbm, tok),
+                (up_first_hbm, up_first), (up_second_hbm, up_second),
+                (first_hbm, first), (second_hbm, second),
+            )
         )
     ]
     for c in locals_:
@@ -90,7 +101,9 @@
         barrier, inc=1, device_id={"dp": ahead(k)}, device_id_type=MESH))
     pl.semaphore_signal(barrier, inc=1, device_id={"sub": other}, device_id_type=MESH)
 
+    locals_[0].wait()
     up_all[me] = up[...].astype(bf16)
+    locals_[1].wait()
     for m in range(2):
         down_all[me, m] = down[:, m, :].astype(bf16)
 
@@ -105,9 +118,18 @@
         to_learner(DOWN, k, block, block).start()
 
     loop(1, n, send_up)
-    loop(1, n, send_down)
-
-    locals_[0].wait()
+    if relayed:
+        send_down(2)
+        for k in (toward, near):
+            pl.when(jnp.logical_or(middle, k != toward))(functools.partial(send_down, k))
+
+        @pl.when(jnp.logical_not(middle))
+        def _():
+            grad_recv[near] = jnp.zeros(grad_recv.shape[1:], bf16)
+    else:
+        loop(1, n, send_down)
+
+    locals_[2].wait()
     for m in range(2):
         cot[m] = cot_raw[:, m, :]
 
@@ -134,7 +156,7 @@
         for q in range(n):
             back[q, m] = total[q * rows:(q + 1) * rows]
 
-    locals_[1].wait()
+    locals_[3].wait()
 
     def grad_for(q):
         lhs = back[q].reshape(2 * rows, tok.shape[0])
@@ -147,7 +169,28 @@
         grad_send[k, 1] = g[rows:]
         to_learner(GRAD_DOWN, k, grad_send.at[k], grad_recv.at[k]).start()
 
-    loop(1, n, send_grad)
+    if relayed:
+        relay_in = pltpu.make_async_remote_copy(
+            src_ref=grad_send.at[0], dst_ref=grad_relay,
+            send_sem=sems.at[RELAY, 0, 0], recv_sem=sems.at[RELAY, 1, 0],
+            device_id={"dp": beside}, device_id_type=MESH,
+        )
+
+        @pl.when(middle)
+        def _():
+            send_grad(toward)
+            send_grad(near)
+
+        @pl.when(jnp.logical_not(middle))
+        def _():
+            g = grad_for(ahead(toward)).astype(bf16)
+            grad_send[0, 0] = g[:rows]
+            grad_send[0, 1] = g[rows:]
+            relay_in.start()
+            send_grad(2)
+            send_grad(near)
+    else:
+        loop(1, n, send_grad)
     g = grad_for(me)
     grad_own[0] = g[:rows]
     grad_own[1] = g[rows:]
@@ -168,7 +211,30 @@
         to_learner(DOWN, k, block, block).wait_recv()
         low_for(q)
 
-    loop(1, n, take_down)
+    down_relay = None
+    if relayed:
+        take_down(2)
+        block = down_all.at[behind(2)]
+        down_relay = pltpu.make_async_remote_copy(
+            src_ref=block, dst_ref=block,
+            send_sem=sems.at[RELAY, 0, 1], recv_sem=sems.at[DOWN, 1, lax.rem(2 * me + 3, 4)],
+            device_id={"dp": beside}, device_id_type=MESH,
+        )
+
+        @pl.when(middle)
+        def _():
+            down_relay.start()
+            g = grad_for(ahead(2))
+            relay_in.wait_recv()
+            for m in range(2):
+                grad_send[2, m] = (
+                    g[m * rows:(m + 1) * rows] + grad_relay[m].astype(f32)).astype(bf16)
+            to_learner(GRAD_DOWN, 2, grad_send.at[2], grad_recv.at[2]).start()
+
+        take_down(toward)
+        take_down(near)
+    else:
+        loop(1, n, take_down)
     half = to_core(LOW, 0, low_send.at[other], low_recv)
     half.start()
     half.wait()
@@ -187,6 +253,8 @@
         gu_own[n] = gu_own[n] + gu_recv[k].astype(f32)
 
     loop(1, n, add_up)
+    locals_[4].wait()
+    locals_[5].wait()
     p, f, s = apply_adam_rule(up[core], up_first[core], up_second[core], gu_own[n])
     up_new_all[me, core] = p.astype(bf16)
 
@@ -201,10 +269,18 @@
     mine = to_core(STATE, 0, state.at[core], state.at[core])
     mine.start()
 
-    locals_[2].wait()
-    locals_[3].wait()
-    loop(1, n, lambda k: to_learner(
-        GRAD_DOWN, k, grad_send.at[k], grad_recv.at[k]).wait_recv())
+    locals_[6].wait()
+    locals_[7].wait()
+
+    def got_grad(k):
+        to_learner(GRAD_DOWN, k, grad_send.at[k], grad_recv.at[k]).wait_recv()
+
+    if relayed:
+        got_grad(2)
+        got_grad(toward)
+        pl.when(middle)(functools.partial(got_grad, near))
+    else:
+        loop(1, n, got_grad)
 
     def adam_down(k):
         q = ahead(k)
@@ -264,9 +340,6 @@
         to_learner(UP, k, block, block).wait_send()
         block = up_all.at[behind(k), core]
         to_core(UP_CROSS, k, block, block).wait_send()
-        block = down_all.at[me]
-        to_learner(DOWN, k, block, block).wait_send()
-        to_learner(GRAD_DOWN, k, grad_send.at[k], grad_recv.at[k]).wait_send()
         to_learner(GRAD_UP, k, gu_send.at[ahead(k)], gu_recv.at[k]).wait_send()
         block = up_new_all.at[me, core]
         to_learner(NEW_UP, k, block, block).wait_send()
@@ -274,7 +347,26 @@
         to_core(NEW_UP_CROSS, k, block, block).wait_send()
         to_learner(COLUMNS, k, col_send.at[k], col_all.at[me]).wait_send()
 
+    def sent_down(k):
+        block = down_all.at[me]
+        to_learner(DOWN, k, block, block).wait_send()
+        to_learner(GRAD_DOWN, k, grad_send.at[k], grad_recv.at[k]).wait_send()
+
     loop(1, n, sent)
+    if relayed:
+        sent_down(2)
+        sent_down(near)
+
+        @pl.when(middle)
+        def _():
+            sent_down(toward)
+            down_relay.wait_send()
+
+        @pl.when(jnp.logical_not(middle))
+        def _():
+            relay_in.wait_send()
+    else:
+        loop(1, n, sent_down)
     mine.wait_send()
 
 
@@ -336,7 +428,7 @@
             jax.ShapeDtypeStruct((2, rank, w), bf16),
             jax.ShapeDtypeStruct((2, rank, o), bf16),
         ),
-        in_specs=[anywhere, anywhere, vmem, anywhere, anywhere, vmem, vmem, vmem],
+        in_specs=[pl.BlockSpec(memory_space=pltpu.HBM)] * 8,
         out_specs=(vmem,) * 8,
         scratch_shapes=[
             pltpu.VMEM((t, d), bf16),
@@ -344,6 +436,10 @@
             pltpu.VMEM((2, t, o), bf16),
             pltpu.VMEM((r, 2, d), f32),
             pltpu.VMEM((r, 2, d), f32),
+            pltpu.VMEM((r, 2, d), f32),
+            pltpu.VMEM((2, rank, c), f32),
+            pltpu.VMEM((2, rank, c), f32),
+            pltpu.VMEM((2, rank, c), f32),
             pltpu.VMEM((n, 2, rank, c), bf16),
             pltpu.VMEM((n, 2, r, d), bf16),
             pltpu.VMEM((n, 2, r, t), bf16),
@@ -360,8 +456,9 @@
             pltpu.VMEM((2, 3, rank, c), f32),
             pltpu.VMEM((n, 2, r, w), bf16),
             pltpu.VMEM((n, 2, r, w), bf16),
+            pltpu.VMEM((2, r, d), bf16),
             pltpu.SemaphoreType.DMA((KINDS, 2, n)),
-            pltpu.SemaphoreType.DMA((4,)),
+            pltpu.SemaphoreType.DMA((8,)),
         ],
         compiler_params=pltpu.CompilerParams(
             collective_id=0, has_side_effects=True, vmem_limit_bytes=48 * 1024 * 1024

time: 79.3 us -> 68.7 us (0.87)
  Pallas kernels: 70.9 us -> 60.3 us
    pallas_call x1, Pallas kernels: 65.6 us -> 55.1 us  [local(): pl.pallas_call(functools.partial(exchange_kernel, n), out_shape=(down_lik...]
where the time goes in v2:
time: 68.7 us; the launch traced here: 68.4 us
  Pallas kernels  60.3 us (88%)
  local copies, waits for them, and re-layouts  7.4 us (11%)
    pallas_call x1, Pallas kernels, local(): pl.pallas_call(functools.partial(exchange_kernel, n), out_shape=(down_lik...  55.1 us
    unnamed x16, local copies, waits for them, and re-layouts  7.4 us
    pallas_call x1, Pallas kernels, local(): pl.pallas_call(merge_kernel, grid=(2, o // block), out_shape=(jax.ShapeDt...  5.29 us

profile of v2, /device:TPU:0, one launch (start us, length us, event | category | flops | bytes accessed | tf_op | source)
XLA Modules:
  0.0 68.4 jit_solution(12078854332988780659)
XLA Ops:
  0.6 0.0 copy-start
  0.6 0.0 copy-start.1
  0.7 1.4 %copy-done.1 = bf16[1,256,2,1024]{3,2,1,0:T(2,128)(2,1)S(1)} copy-done((bf16[1,256,2,1024]{3,2,1,0:T(2,128)(2,1)S(1)}, bf16[1,256,2,1024]{3,2,1,0:T(2,128)(2,1)}, u32[]{:S(2)}) %copy-start.1) | copy-done | bytes 1048600
  2.0 0.0 copy-start.2
  2.0 1.2 %copy-done.2 = f32[1,16,2,4096]{3,2,1,0:T(2,128)S(1)} copy-done((f32[1,16,2,4096]{3,2,1,0:T(2,128)S(1)}, f32[1,16,2,4096]{3,2,1,0:T(2,128)}, u32[]{:S(2)}) %copy-start.2) | copy-done | bytes 524312
  3.3 0.0 copy-start.3
  3.3 1.0 %copy-done.3 = f32[1,16,2,4096]{3,2,1,0:T(2,128)S(1)} copy-done((f32[1,16,2,4096]{3,2,1,0:T(2,128)S(1)}, f32[1,16,2,4096]{3,2,1,0:T(2,128)}, u32[]{:S(2)}) %copy-start.3) | copy-done | bytes 524312
  4.3 0.0 copy-start.4
  4.3 1.0 %copy-done.4 = f32[1,16,2,4096]{3,2,1,0:T(2,128)S(1)} copy-done((f32[1,16,2,4096]{3,2,1,0:T(2,128)S(1)}, f32[1,16,2,4096]{3,2,1,0:T(2,128)}, u32[]{:S(2)}) %copy-start.4) | copy-done | bytes 524312
  5.3 0.0 copy-start.5
  5.3 0.9 %copy-done.5 = f32[1,256,2,64]{1,3,2,0:T(8,128)S(1)} copy-done((f32[1,256,2,64]{1,3,2,0:T(8,128)S(1)}, f32[1,256,2,64]{1,3,2,0:T(8,128)}, u32[]{:S(2)}) %copy-start.5) | copy-done | bytes 131096
  6.2 0.0 copy-start.6
  6.2 0.9 %copy-done.6 = f32[1,256,2,64]{1,3,2,0:T(8,128)S(1)} copy-done((f32[1,256,2,64]{1,3,2,0:T(8,128)S(1)}, f32[1,256,2,64]{1,3,2,0:T(8,128)}, u32[]{:S(2)}) %copy-start.6) | copy-done | bytes 131096
  7.1 0.0 copy-start.7
  7.2 0.9 %copy-done.7 = f32[1,256,2,64]{1,3,2,0:T(8,128)S(1)} copy-done((f32[1,256,2,64]{1,3,2,0:T(8,128)S(1)}, f32[1,256,2,64]{1,3,2,0:T(8,128)}, u32[]{:S(2)}) %copy-start.7) | copy-done | bytes 131096
  8.1 55.1 %shard_map.144 = (f32[16,2,4096]{2,1,0:T(2,128)S(1)}, f32[16,2,4096]{2,1,0:T(2,128)S(1)}, f32[16,2,4096]{2,1,0:T(2,128)S(1)}, f32[2,64,256]{2,1,0:T(8,128)S(1)},...) custom-call(bf16[256,4096]{1,0:T(8,128)(2,1)} %bitcast.36, ...), custom_call_target="tpu_custom_call" | custom-call | flops 1000000000 | bytes 10000000 | tf_op jit(solution)/shard_map/pallas_call | solution.py:424
  63.1 0.0 copy-done
  63.1 5.3 %shard_map.145 = (bf16[2,1024,1024]{2,1,0:T(8,128)(2,1)}, f32[16,2,4096]{2,1,0:T(2,128)}, f32[16,2,4096]{2,1,0:T(2,128)}, f32[16,2,4096]{2,1,0:T(2,128)}, f32[2,...) custom-call(bf16[2,1024,1024]{2,1,0:T(8,128)(2,1)S(1)} %bitcast.28, ...), custom_call_target="tpu_custom_call" | custom-call | tf_op jit(solution)/shard_map/pallas_call | solution.py:470
Async XLA Ops:
  0.6 62.5 %copy-start = (bf16[1,2,1024,1024]{3,2,1,0:T(8,128)(2,1)S(1)}, bf16[1,2,1024,1024]{3,2,1,0:T(8,128)(2,1)}, u32[]{:S(2)}) copy-start(bf16[1,2,1024,1024]{3,2,1,0:T(8,128)(2,1)} %param.11) | copy-start | bytes 12582916
  0.6 1.4 %copy-start.1 = (bf16[1,256,2,1024]{3,2,1,0:T(2,128)(2,1)S(1)}, bf16[1,256,2,1024]{3,2,1,0:T(2,128)(2,1)}, u32[]{:S(2)}) copy-start(bf16[1,256,2,1024]{3,2,1,0:T(2,128)(2,1)} %param.10) | copy-start | bytes 3145732
  2.0 1.2 %copy-start.2 = (f32[1,16,2,4096]{3,2,1,0:T(2,128)S(1)}, f32[1,16,2,4096]{3,2,1,0:T(2,128)}, u32[]{:S(2)}) copy-start(f32[1,16,2,4096]{3,2,1,0:T(2,128)} %param.12) | copy-start | bytes 1572868
  3.3 1.0 %copy-start.3 = (f32[1,16,2,4096]{3,2,1,0:T(2,128)S(1)}, f32[1,16,2,4096]{3,2,1,0:T(2,128)}, u32[]{:S(2)}) copy-start(f32[1,16,2,4096]{3,2,1,0:T(2,128)} %param.13) | copy-start | bytes 1572868
  4.3 1.0 %copy-start.4 = (f32[1,16,2,4096]{3,2,1,0:T(2,128)S(1)}, f32[1,16,2,4096]{3,2,1,0:T(2,128)}, u32[]{:S(2)}) copy-start(f32[1,16,2,4096]{3,2,1,0:T(2,128)} %param.14) | copy-start | bytes 1572868
  5.3 0.9 %copy-start.5 = (f32[1,256,2,64]{1,3,2,0:T(8,128)S(1)}, f32[1,256,2,64]{1,3,2,0:T(8,128)}, u32[]{:S(2)}) copy-start(f32[1,256,2,64]{1,3,2,0:T(8,128)} %param.15) | copy-start | bytes 393220
  6.2 0.9 %copy-start.6 = (f32[1,256,2,64]{1,3,2,0:T(8,128)S(1)}, f32[1,256,2,64]{1,3,2,0:T(8,128)}, u32[]{:S(2)}) copy-start(f32[1,256,2,64]{1,3,2,0:T(8,128)} %param.16) | copy-start | bytes 393220
  7.1 0.9 %copy-start.7 = (f32[1,256,2,64]{1,3,2,0:T(8,128)S(1)}, f32[1,256,2,64]{1,3,2,0:T(8,128)}, u32[]{:S(2)}) copy-start(f32[1,256,2,64]{1,3,2,0:T(8,128)} %param.17) | copy-start | bytes 393220

commit v3 on v2

--- a/solution.py
+++ b/solution.py
@@ -35,16 +35,16 @@
     n,
     tok_hbm, cot_hbm, down_hbm, first_hbm, second_hbm, up_hbm, up_first_hbm, up_second_hbm,
     new_down, new_first, new_second, new_up, new_up_first, new_up_second, columns_out, up_out,
-    tok, cot_raw, cot, down, first, second, up, up_first, up_second,
+    tok, cot_raw, cot, down_raw, first_raw, second_raw, down, first, second, up, up_first, up_second,
     up_all, down_all, back, grad_send, grad_recv, grad_own,
     low_own, low_send, low_recv, gu_send, gu_recv, gu_own, up_new_all, state, col_send, col_all,
-    grad_relay, sems, local_sems,
+    grad_relay, sems, local_sems, out_sems,
 ):
     bf16, f32 = jnp.bfloat16, jnp.float32
     me = lax.axis_index("dp")
     core = lax.axis_index("sub")
     other = 1 - core
-    rows = down.shape[0]
+    rows = down.shape[1]
     rank = up.shape[1]
     kv_rows = up.shape[2]
     width = down.shape[2] // n
@@ -87,9 +87,9 @@
         pltpu.make_async_copy(src, dst, local_sems.at[i])
         for i, (src, dst) in enumerate(
             (
-                (up_hbm, up), (down_hbm, down), (cot_hbm, cot_raw), (tok_hbm, tok),
+                (up_hbm, up), (down_hbm, down_raw), (cot_hbm, cot_raw), (tok_hbm, tok),
                 (up_first_hbm, up_first), (up_second_hbm, up_second),
-                (first_hbm, first), (second_hbm, second),
+                (first_hbm, first_raw), (second_hbm, second_raw),
             )
         )
     ]
@@ -103,10 +103,6 @@
 
     locals_[0].wait()
     up_all[me] = up[...].astype(bf16)
-    locals_[1].wait()
-    for m in range(2):
-        down_all[me, m] = down[:, m, :].astype(bf16)
-
     pl.semaphore_wait(barrier, n)
 
     def send_up(k):
@@ -118,6 +114,10 @@
         to_learner(DOWN, k, block, block).start()
 
     loop(1, n, send_up)
+    locals_[1].wait()
+    for m in range(2):
+        down[m] = down_raw[:, m, :]
+        down_all[me, m] = down[m].astype(bf16)
     if relayed:
         send_down(2)
         for k in (toward, near):
@@ -194,6 +194,11 @@
     g = grad_for(me)
     grad_own[0] = g[:rows]
     grad_own[1] = g[rows:]
+    locals_[6].wait()
+    locals_[7].wait()
+    for m in range(2):
+        first[m] = first_raw[:, m, :]
+        second[m] = second_raw[:, m, :]
 
     def low_for(q):
         part = lax.dot_general(
@@ -269,9 +274,6 @@
     mine = to_core(STATE, 0, state.at[core], state.at[core])
     mine.start()
 
-    locals_[6].wait()
-    locals_[7].wait()
-
     def got_grad(k):
         to_learner(GRAD_DOWN, k, grad_send.at[k], grad_recv.at[k]).wait_recv()
 
@@ -289,10 +291,10 @@
             g = grad_own[m, :, cols]
             for j in range(1, n):
                 g = g + grad_recv[j, m, :, cols].astype(f32)
-            p, f, s = apply_adam_rule(down[:, m, cols], first[:, m, cols], second[:, m, cols], g)
-            new_down[:, m, cols] = p
-            new_first[:, m, cols] = f
-            new_second[:, m, cols] = s
+            p, f, s = apply_adam_rule(down[m, :, cols], first[m, :, cols], second[m, :, cols], g)
+            down[m, :, cols] = p
+            first[m, :, cols] = f
+            second[m, :, cols] = s
             if isinstance(k, int) and k == 0:
                 col_all[me, m] = p.astype(bf16)
             else:
@@ -302,7 +304,12 @@
         adam_down(k)
         to_learner(COLUMNS, k, col_send.at[k], col_all.at[me]).start()
 
-    loop(1, n, send_columns)
+    if relayed:
+        send_columns(2)
+        send_columns(toward)
+        send_columns(near)
+    else:
+        loop(1, n, send_columns)
     adam_down(0)
 
     def pass_new_up(k):
@@ -311,29 +318,37 @@
         to_core(NEW_UP_CROSS, k, block, block).start()
 
     loop(1, n, pass_new_up)
+    outputs = []
+
+    def write_out(src, dst):
+        outputs.append(pltpu.make_async_copy(src, dst, out_sems.at[len(outputs)]))
+        outputs[-1].start()
+
     to_core(STATE, 0, state.at[other], state.at[other]).wait_recv()
     for m in range(2):
-        new_up[m] = state[m, 0]
-        new_up_first[m] = state[m, 1]
-        new_up_second[m] = state[m, 2]
+        for i, out in enumerate((new_up, new_up_first, new_up_second)):
+            write_out(state.at[m, i], out.at[m])
     up_new_all[me, other] = state[other, 0].astype(bf16)
+
+    for new, raw, out in (
+        (down, down_raw, new_down), (first, first_raw, new_first), (second, second_raw, new_second)
+    ):
+        for m in range(2):
+            raw[:, m, :] = new[m]
+        write_out(raw, out)
 
     def got_new_up(k):
         block = up_new_all.at[behind(k), other]
         to_core(NEW_UP_CROSS, k, block, block).wait_recv()
 
     loop(1, n, got_new_up)
-    for m in range(2):
-        for q in range(n):
-            up_out[m, :, q * kv_rows:(q + 1) * kv_rows] = up_new_all[q, m]
+    write_out(up_new_all, up_out)
 
     def got_columns(k):
         to_learner(COLUMNS, k, col_send.at[k], col_all.at[behind(k)]).wait_recv()
 
     loop(1, n, got_columns)
-    for m in range(2):
-        for q in range(n):
-            columns_out[m, q * rows:(q + 1) * rows, :] = col_all[q, m]
+    write_out(col_all, columns_out)
 
     def sent(k):
         block = up_all.at[me, core]
@@ -368,6 +383,8 @@
     else:
         loop(1, n, sent_down)
     mine.wait_send()
+    for c in outputs:
+        c.wait()
 
 
 def merge_kernel(
@@ -384,9 +401,11 @@
         for c in copies:
             c.start()
 
+    n, _, rows, width = columns.shape
     change = lax.dot_general(
-        up[0], columns[0], (((0,), (0,)), ((), ())), preferred_element_type=jnp.float32)
-    merged[0] = (frozen[0].astype(jnp.float32) + adapter_scale * change).astype(merged.dtype)
+        adapter_scale * up[0, 0], columns[:, 0].reshape(n * rows, width),
+        (((0,), (0,)), ((), ())), preferred_element_type=jnp.float32)
+    merged[0] = (frozen[0].astype(jnp.float32) + change).astype(merged.dtype)
 
     @pl.when(step == last)
     def _():
@@ -417,19 +436,18 @@
     r = down.shape[0]
     rank, c = up.shape[1:]
     w = d // n
-    vmem = pl.BlockSpec(memory_space=pltpu.VMEM)
-    anywhere = pl.BlockSpec(memory_space=pl.ANY)
+    hbm = pl.BlockSpec(memory_space=pltpu.HBM)
     down_like = jax.ShapeDtypeStruct(down.shape, f32)
     up_like = jax.ShapeDtypeStruct(up.shape, f32)
     outs = pl.pallas_call(
         functools.partial(exchange_kernel, n),
         out_shape=(
             down_like, down_like, down_like, up_like, up_like, up_like,
-            jax.ShapeDtypeStruct((2, rank, w), bf16),
-            jax.ShapeDtypeStruct((2, rank, o), bf16),
+            jax.ShapeDtypeStruct((n, 2, r, w), bf16),
+            jax.ShapeDtypeStruct((n, 2, rank, c), bf16),
         ),
-        in_specs=[pl.BlockSpec(memory_space=pltpu.HBM)] * 8,
-        out_specs=(vmem,) * 8,
+        in_specs=[hbm] * 8,
+        out_specs=(hbm,) * 8,
         scratch_shapes=[
             pltpu.VMEM((t, d), bf16),
             pltpu.VMEM((t, 2, o), bf16),
@@ -437,6 +455,9 @@
             pltpu.VMEM((r, 2, d), f32),
             pltpu.VMEM((r, 2, d), f32),
             pltpu.VMEM((r, 2, d), f32),
+            pltpu.VMEM((2, r, d), f32),
+            pltpu.VMEM((2, r, d), f32),
+            pltpu.VMEM((2, r, d), f32),
             pltpu.VMEM((2, rank, c), f32),
             pltpu.VMEM((2, rank, c), f32),
             pltpu.VMEM((2, rank, c), f32),
@@ -459,29 +480,29 @@
             pltpu.VMEM((2, r, d), bf16),
             pltpu.SemaphoreType.DMA((KINDS, 2, n)),
             pltpu.SemaphoreType.DMA((8,)),
+            pltpu.SemaphoreType.DMA((11,)),
         ],
         compiler_params=pltpu.CompilerParams(
-            collective_id=0, has_side_effects=True, vmem_limit_bytes=48 * 1024 * 1024
+            collective_id=0, has_side_effects=True, vmem_limit_bytes=60 * 1024 * 1024
         ),
         cost_estimate=pl.CostEstimate(flops=10**9, bytes_accessed=10**7, transcendentals=0),
     )(tok, cot, down, first, second, up, up_first, up_second)
     columns, up_cast = outs[6], outs[7]
-    block = min(256, o)
     merged, *rest = pl.pallas_call(
         merge_kernel,
-        grid=(2, o // block),
+        grid=(2, n),
         out_shape=(
             jax.ShapeDtypeStruct((2, o, w), bf16),
             down_like, down_like, down_like, up_like, up_like, up_like,
         ),
         in_specs=[
-            pl.BlockSpec((1, block, w), lambda m, i: (m, i, 0)),
-            pl.BlockSpec((1, rank, block), lambda m, i: (m, 0, i)),
-            pl.BlockSpec((1, rank, w), lambda m, i: (m, 0, 0)),
-        ] + [anywhere] * 6,
-        out_specs=(pl.BlockSpec((1, block, w), lambda m, i: (m, i, 0)),) + (anywhere,) * 6,
+            pl.BlockSpec((1, c, w), lambda m, i: (m, i, 0)),
+            pl.BlockSpec((1, 1, rank, c), lambda m, i: (i, m, 0, 0)),
+            pl.BlockSpec((n, 1, r, w), lambda m, i: (0, m, 0, 0)),
+        ] + [hbm] * 6,
+        out_specs=(pl.BlockSpec((1, c, w), lambda m, i: (m, i, 0)),) + (hbm,) * 6,
         scratch_shapes=[pltpu.SemaphoreType.DMA((6,))],
-        compiler_params=pltpu.CompilerParams(vmem_limit_bytes=32 * 1024 * 1024),
+        compiler_params=pltpu.CompilerParams(vmem_limit_bytes=60 * 1024 * 1024),
     )(frozen, up_cast, columns, *outs[:6])
     return (
         merged[None],

time: 68.7 us -> 119 us (1.73)
  Pallas kernels: 60.3 us -> 118 us
  local copies, waits for them, and re-layouts: 7.4 us -> 0 us
    pallas_call x1, Pallas kernels: 5.29 us -> 62.6 us  [local(): pl.pallas_call(merge_kernel, grid=(2, n), out_shape=(jax.ShapeDtypeStruct...]
    unnamed x16 -> x0, local copies, waits for them, and re-layouts: 7.4 us -> none
where the time goes in v3:
time: 119 us; the launch traced here: 118 us
  Pallas kernels  118 us (99%)
    pallas_call x1, Pallas kernels, local(): pl.pallas_call(merge_kernel, grid=(2, n), out_shape=(jax.ShapeDtypeStruct...  62.6 us
    pallas_call x1, Pallas kernels, local(): pl.pallas_call(functools.partial(exchange_kernel, n), out_shape=(down_lik...  55.2 us

profile of v3, /device:TPU:0, one launch (start us, length us, event | category | flops | bytes accessed | tf_op | source)
XLA Modules:
  0.0 118.5 jit_solution(6463513113630666180)
XLA Ops:
  0.6 55.2 %shard_map.144 = (f32[16,2,4096]{2,1,0:T(2,128)}, f32[16,2,4096]{2,1,0:T(2,128)}, f32[16,2,4096]{2,1,0:T(2,128)}, f32[2,64,256]{2,1,0:T(8,128)}, f32[2,64,256]{2...) custom-call(bf16[256,4096]{1,0:T(8,128)(2,1)} %bitcast.29, ...), custom_call_target="tpu_custom_call" | custom-call | flops 1000000000 | bytes 10000000 | tf_op jit(solution)/shard_map/pallas_call | solution.py:442
  55.8 62.6 %shard_map.145 = (bf16[2,1024,1024]{2,1,0:T(8,128)(2,1)}, f32[16,2,4096]{2,1,0:T(2,128)}, f32[16,2,4096]{2,1,0:T(2,128)}, f32[16,2,4096]{2,1,0:T(2,128)}, f32[2,...) custom-call(bf16[2,1024,1024]{2,1,0:T(8,128)(2,1)} %bitcast.28, ...), custom_call_target="tpu_custom_call" | custom-call | tf_op jit(solution)/shard_map/pallas_call | solution.py:491

commit v4 on v3

--- a/solution.py
+++ b/solution.py
@@ -389,17 +389,29 @@
 
 def merge_kernel(
     frozen, up, columns, d0, d1, d2, u0, u1, u2,
-    merged, e0, e1, e2, v0, v1, v2, sems,
+    merged, e0, e1, e2, v0, v1, v2, b0, b1, b2, b3, b4, b5, sems,
 ):
     step = pl.program_id(0) * pl.num_programs(1) + pl.program_id(1)
     last = pl.num_programs(0) * pl.num_programs(1) - 1
-    pairs = ((d0, e0), (d1, e1), (d2, e2), (u0, v0), (u1, v1), (u2, v2))
-    copies = [pltpu.make_async_copy(a, b, sems.at[i]) for i, (a, b) in enumerate(pairs)]
+    loads = [
+        pltpu.make_async_copy(a, b, sems.at[0, i])
+        for i, (a, b) in enumerate(((d0, b0), (d1, b1), (d2, b2), (u0, b3), (u1, b4), (u2, b5)))
+    ]
+    stores = [
+        pltpu.make_async_copy(b, a, sems.at[1, i])
+        for i, (a, b) in enumerate(((e0, b0), (e1, b1), (e2, b2), (v0, b3), (v1, b4), (v2, b5)))
+    ]
 
     @pl.when(step == 0)
     def _():
-        for c in copies:
+        for c in loads:
             c.start()
+
+    @pl.when(step == 1)
+    def _():
+        for c, e in zip(loads, stores):
+            c.wait()
+            e.start()
 
     n, _, rows, width = columns.shape
     change = lax.dot_general(
@@ -409,7 +421,7 @@
 
     @pl.when(step == last)
     def _():
-        for c in copies:
+        for c in stores:
             c.wait()
 
 
@@ -501,7 +513,9 @@
             pl.BlockSpec((n, 1, r, w), lambda m, i: (0, m, 0, 0)),
         ] + [hbm] * 6,
         out_specs=(pl.BlockSpec((1, c, w), lambda m, i: (m, i, 0)),) + (hbm,) * 6,
-        scratch_shapes=[pltpu.SemaphoreType.DMA((6,))],
+        scratch_shapes=[pltpu.VMEM(down.shape, f32)] * 3 + [pltpu.VMEM(up.shape, f32)] * 3 + [
+            pltpu.SemaphoreType.DMA((2, 6))
+        ],
         compiler_params=pltpu.CompilerParams(vmem_limit_bytes=60 * 1024 * 1024),
     )(frozen, up_cast, columns, *outs[:6])
     return (

time: 119 us -> 65 us (0.55)
  Pallas kernels: 118 us -> 64 us
    pallas_call x1, Pallas kernels: 62.6 us -> 8.85 us  [local(): pl.pallas_call(merge_kernel, grid=(2, n), out_shape=(jax.ShapeDtypeStruct...]
where the time goes in v4:
time: 65 us; the launch traced here: 64.7 us
  Pallas kernels  64 us (98%)
    pallas_call x1, Pallas kernels, local(): pl.pallas_call(functools.partial(exchange_kernel, n), out_shape=(down_lik...  55.2 us
    pallas_call x1, Pallas kernels, local(): pl.pallas_call(merge_kernel, grid=(2, n), out_shape=(jax.ShapeDtypeStruct...  8.85 us

profile of v4, /device:TPU:0, one launch (start us, length us, event | category | flops | bytes accessed | tf_op | source)
XLA Modules:
  0.0 64.7 jit_solution(15636677425772957983)
XLA Ops:
  0.6 55.2 %shard_map.144 = (f32[16,2,4096]{2,1,0:T(2,128)}, f32[16,2,4096]{2,1,0:T(2,128)}, f32[16,2,4096]{2,1,0:T(2,128)}, f32[2,64,256]{2,1,0:T(8,128)}, f32[2,64,256]{2...) custom-call(bf16[256,4096]{1,0:T(8,128)(2,1)} %bitcast.29, ...), custom_call_target="tpu_custom_call" | custom-call | flops 1000000000 | bytes 10000000 | tf_op jit(solution)/shard_map/pallas_call | solution.py:454
  55.8 8.8 %shard_map.145 = (bf16[2,1024,1024]{2,1,0:T(8,128)(2,1)}, f32[16,2,4096]{2,1,0:T(2,128)}, f32[16,2,4096]{2,1,0:T(2,128)}, f32[16,2,4096]{2,1,0:T(2,128)}, f32[2,...) custom-call(bf16[2,1024,1024]{2,1,0:T(8,128)(2,1)} %bitcast.28, ...), custom_call_target="tpu_custom_call" | custom-call | tf_op jit(solution)/shard_map/pallas_call | solution.py:503

commit v5 on v3

--- a/solution.py
+++ b/solution.py
@@ -389,28 +389,49 @@
 
 def merge_kernel(
     frozen, up, columns, d0, d1, d2, u0, u1, u2,
-    merged, e0, e1, e2, v0, v1, v2, sems,
+    merged, e0, e1, e2, v0, v1, v2,
+    start, result, up_in, cols_in, b0, b1, b2, b3, b4, b5, load_sems, store_sems, sems,
 ):
-    step = pl.program_id(0) * pl.num_programs(1) + pl.program_id(1)
-    last = pl.num_programs(0) * pl.num_programs(1) - 1
-    pairs = ((d0, e0), (d1, e1), (d2, e2), (u0, v0), (u1, v1), (u2, v2))
-    copies = [pltpu.make_async_copy(a, b, sems.at[i]) for i, (a, b) in enumerate(pairs)]
-
-    @pl.when(step == 0)
-    def _():
-        for c in copies:
-            c.start()
-
     n, _, rows, width = columns.shape
-    change = lax.dot_general(
-        adapter_scale * up[0, 0], columns[:, 0].reshape(n * rows, width),
-        (((0,), (0,)), ((), ())), preferred_element_type=jnp.float32)
-    merged[0] = (frozen[0].astype(jnp.float32) + change).astype(merged.dtype)
-
-    @pl.when(step == last)
-    def _():
-        for c in copies:
-            c.wait()
+    rank, block = up.shape[2:]
+    factors = [
+        pltpu.make_async_copy(up, up_in, sems.at[2, 0]),
+        pltpu.make_async_copy(columns, cols_in, sems.at[2, 1]),
+    ]
+    pieces = [(m, q) for m in range(2) for q in range(n)]
+    loads, stores = [], []
+    for m, q in pieces:
+        part = pl.ds(q * block, block)
+        loads.append(pltpu.make_async_copy(
+            frozen.at[m, part], start.at[m, q], load_sems.at[m, q]))
+        stores.append(pltpu.make_async_copy(
+            result.at[m, q], merged.at[m, part], store_sems.at[m, q]))
+    held = (b0, b1, b2, b3, b4, b5)
+    ins = [
+        pltpu.make_async_copy(a, b, sems.at[0, i])
+        for i, (a, b) in enumerate(zip((d0, d1, d2, u0, u1, u2), held))
+    ]
+    outs = [
+        pltpu.make_async_copy(b, a, sems.at[1, i])
+        for i, (a, b) in enumerate(zip((e0, e1, e2, v0, v1, v2), held))
+    ]
+    for c in factors + loads[:2] + ins + loads[2:]:
+        c.start()
+    for c in factors:
+        c.wait()
+    for i, (m, q) in enumerate(pieces):
+        change = lax.dot_general(
+            adapter_scale * up_in[q, m], cols_in[:, m].reshape(n * rows, width),
+            (((0,), (0,)), ((), ())), preferred_element_type=jnp.float32)
+        loads[i].wait()
+        result[m, q] = (start[m, q].astype(jnp.float32) + change).astype(result.dtype)
+        stores[i].start()
+        if i == 1:
+            for c, e in zip(ins, outs):
+                c.wait()
+                e.start()
+    for c in stores + outs:
+        c.wait()
 
 
 def local(
@@ -490,18 +511,22 @@
     columns, up_cast = outs[6], outs[7]
     merged, *rest = pl.pallas_call(
         merge_kernel,
-        grid=(2, n),
         out_shape=(
             jax.ShapeDtypeStruct((2, o, w), bf16),
             down_like, down_like, down_like, up_like, up_like, up_like,
         ),
-        in_specs=[
-            pl.BlockSpec((1, c, w), lambda m, i: (m, i, 0)),
-            pl.BlockSpec((1, 1, rank, c), lambda m, i: (i, m, 0, 0)),
-            pl.BlockSpec((n, 1, r, w), lambda m, i: (0, m, 0, 0)),
-        ] + [hbm] * 6,
-        out_specs=(pl.BlockSpec((1, c, w), lambda m, i: (m, i, 0)),) + (hbm,) * 6,
-        scratch_shapes=[pltpu.SemaphoreType.DMA((6,))],
+        in_specs=[hbm] * 9,
+        out_specs=(hbm,) * 7,
+        scratch_shapes=[
+            pltpu.VMEM((2, n, c, w), bf16),
+            pltpu.VMEM((2, n, c, w), bf16),
+            pltpu.VMEM((n, 2, rank, c), bf16),
+            pltpu.VMEM((n, 2, r, w), bf16),
+        ] + [pltpu.VMEM(down.shape, f32)] * 3 + [pltpu.VMEM(up.shape, f32)] * 3 + [
+            pltpu.SemaphoreType.DMA((2, n)),
+            pltpu.SemaphoreType.DMA((2, n)),
+            pltpu.SemaphoreType.DMA((3, 6)),
+        ],
         compiler_params=pltpu.CompilerParams(vmem_limit_bytes=60 * 1024 * 1024),
     )(frozen, up_cast, columns, *outs[:6])
     return (

time: 119 us -> 62.6 us (0.53)
  Pallas kernels: 118 us -> 61.8 us
    pallas_call x1, Pallas kernels: 62.6 us -> 6.61 us  [local(): pl.pallas_call(merge_kernel, out_shape=(jax.ShapeDtypeStruct((2, o, w), b...]
where the time goes in v5:
time: 62.6 us; the launch traced here: 62.4 us
  Pallas kernels  61.8 us (99%)
  between operations  0.64 us (1%)
    pallas_call x1, Pallas kernels, local(): pl.pallas_call(functools.partial(exchange_kernel, n), out_shape=(down_lik...  55.2 us
    pallas_call x1, Pallas kernels, local(): pl.pallas_call(merge_kernel, out_shape=(jax.ShapeDtypeStruct((2, o, w), b...  6.61 us

profile of v5, /device:TPU:0, one launch (start us, length us, event | category | flops | bytes accessed | tf_op | source)
XLA Modules:
  0.0 62.4 jit_solution(18232051801379466317)
XLA Ops:
  0.6 55.2 %shard_map.144 = (f32[16,2,4096]{2,1,0:T(2,128)}, f32[16,2,4096]{2,1,0:T(2,128)}, f32[16,2,4096]{2,1,0:T(2,128)}, f32[2,64,256]{2,1,0:T(8,128)}, f32[2,64,256]{2...) custom-call(bf16[256,4096]{1,0:T(8,128)(2,1)} %bitcast.29, ...), custom_call_target="tpu_custom_call" | custom-call | flops 1000000000 | bytes 10000000 | tf_op jit(solution)/shard_map/pallas_call | solution.py:463
  55.8 6.6 %shard_map.145 = (bf16[2,1024,1024]{2,1,0:T(8,128)(2,1)}, f32[16,2,4096]{2,1,0:T(2,128)}, f32[16,2,4096]{2,1,0:T(2,128)}, f32[16,2,4096]{2,1,0:T(2,128)}, f32[2,...) custom-call(bf16[2,1024,1024]{2,1,0:T(8,128)(2,1)} %bitcast.28, ...), custom_call_target="tpu_custom_call" | custom-call | tf_op jit(solution)/shard_map/pallas_call | solution.py:512
